TPU v7x, 128 devices: a whole 4x4x4 slice. The times are simulated.
128 devices in a mesh: atm: 16 (over z, y), ocn: 8 (over x, core).
Axes of the slice: x: 4, y: 4, z: 4, core: 2. Of those that a mesh axis runs over, the one named last changes fastest.
Arguments:
- atm_fields: bfloat16 [16384, 24, 128], P(('atm', 'ocn')), may hold values from -6 to 6
- fwd_blocks: bfloat16 [24576, 128, 128], P(('atm', 'ocn')), may hold values from -0.21875 to 0.21875
- fwd_src_tile: int32 [24576], P(('atm', 'ocn')), may hold values from 0 to 127
- fwd_dst_dev: int32 [24576, 1], P(('atm', 'ocn')), may hold values from 0 to 127, as said below
- fwd_dst_tile: int32 [24576], P(('atm', 'ocn')), may hold values from 0 to 7
- ocean_state: float32 [1024, 24, 128], P(('atm', 'ocn')), may hold values from -6 to 6
- wet_mask: int32 [1024, 128], P(('atm', 'ocn')), may hold values 0 or 1
- back_blocks: bfloat16 [24576, 128, 128], P(('atm', 'ocn')), may hold values from -0.3125 to 0.3125
- back_src_dev: int32 [24576, 1], P(('atm', 'ocn')), may hold values from 0 to 127, as said below
- back_src_tile: int32 [24576], P(('atm', 'ocn')), may hold values from 0 to 7
- back_dst_tile: int32 [24576], P(('atm', 'ocn')), may hold values from 0 to 127
Outputs:
- ocean_import: float32 [1024, 24, 128], P(('atm', 'ocn'))
- atm_import: float32 [16384, 24, 128], P(('atm', 'ocn'))
Inputs may be any that keep to these rules, and one draw needn't show every extreme that they name: `fwd_dst_dev`: device d has atm index d // 8 and ocn index d % 8; the device named by a block of device b // 192 differs from it by at most one in each index, counted with wrap-around (nine neighbours, itself included). Among the 192 blocks of one device at most 48 name the same device, and on every device exactly one device is named 48 times. `back_src_dev`: device d has atm index d // 8 and ocn index d % 8; the device named by a block of device b // 192 differs from it by at most one in each index, counted with wrap-around (nine neighbours, itself included). Among the 192 blocks of one device at most 48 name the same device, and on every device exactly one device is named 48 times.
All inputs are finite; a program needn't handle non-finite values. No bound on the sum of `wet_mask` on one device may be relied on, other than what follows from the above.
Results may differ from a plain program's by a relative error of at most 0.0022.
Values may be sent and summed in bfloat16 or wider, within the bound.
A program may use at most 128 MiB of HBM per device.

v0:
```python
import jax
import jax.numpy as jnp
from jax import lax
from jax.sharding import PartitionSpec as P


def extended(block, sides, width):
    for axis, dim in sides:
        count = lax.axis_size(axis)
        forward = [(i, i + 1) for i in range(count - 1)]
        forward.append((count - 1, 0))
        backward = [(target, source) for source, target in forward]
        low = lax.ppermute(
            lax.slice_in_dim(block, block.shape[dim] - width, None, axis=dim), axis, forward
        )
        high = lax.ppermute(lax.slice_in_dim(block, 0, width, axis=dim), axis, backward)
        block = jnp.concatenate([low, block, high], axis=dim)
    return block


def rank_within(owner):
    count = owner.shape[0]
    order = jnp.arange(count, dtype=jnp.int32)
    earlier = (owner[:, None] == owner[None, :]) & (order[None, :] < order[:, None])
    return jnp.sum(earlier.astype(jnp.int32), axis=1)


def tile_sums(labels, values, tiles):
    select = (labels[None, :] == jnp.arange(tiles, dtype=jnp.int32)[:, None]).astype(jnp.float32)
    flat = values.reshape(values.shape[0], -1)
    return jnp.dot(
        select, flat, precision=lax.Precision.HIGHEST, preferred_element_type=jnp.float32
    )


def neighbour_steps(owner, n_atmos, n_ocean):
    here_row = lax.axis_index("atm")
    here_col = lax.axis_index("ocn")
    rel_row = (owner // n_ocean - here_row) % n_atmos
    rel_col = (owner % n_ocean - here_col) % n_ocean
    row_step = jnp.where(rel_row == n_atmos - 1, 0, jnp.where(rel_row == 0, 1, 2)).astype(jnp.int32)
    col_step = jnp.where(rel_col == n_ocean - 1, 0, jnp.where(rel_col == 0, 1, 2)).astype(jnp.int32)
    return (row_step, col_step)


def shards(
    atm_fields,
    fwd_blocks,
    fwd_src_tile,
    fwd_dst_dev,
    fwd_dst_tile,
    ocean_state,
    wet_mask,
    back_blocks,
    back_src_dev,
    back_src_tile,
    back_dst_tile,
):
    n_atmos = lax.axis_size("atm")
    n_ocean = lax.axis_size("ocn")
    blocks = fwd_blocks.shape[0]
    slots = blocks // 4
    fields = atm_fields.shape[1]
    cells = atm_fields.shape[2]
    ocean_count = ocean_state.shape[0]
    atmos_count = atm_fields.shape[0]
    row_step, col_step = neighbour_steps(fwd_dst_dev[:, 0], n_atmos, n_ocean)
    neighbour = row_step * 3 + col_step
    sources = atm_fields[fwd_src_tile]
    fwd_part = jnp.einsum("bfi,bij->bfj", sources, fwd_blocks, preferred_element_type=jnp.float32)
    place = neighbour * slots + rank_within(neighbour)
    outgoing = jnp.zeros((9 * slots, fields, cells), jnp.float32).at[place].set(fwd_part)
    labels = jnp.zeros((9 * slots,), jnp.int32).at[place].set(fwd_dst_tile)
    padded, padded_labels = (
        extended(outgoing.reshape(3, 3, slots, fields, cells), (("atm", 0), ("ocn", 1)), 1),
        extended(labels.reshape(3, 3, slots), (("atm", 0), ("ocn", 1)), 1),
    )
    arrived = padded[::2, ::2]
    tile_ids = padded_labels[::2, ::2]
    ocean_import = tile_sums(
        tile_ids.reshape(-1), arrived.reshape(9 * slots, fields, cells), ocean_count
    ).reshape(ocean_count, fields, cells)
    wet = wet_mask.astype(jnp.float32)[:, None, :]
    response = (wet * jnp.tanh(ocean_state + ocean_import)).astype(jnp.bfloat16)
    source_owner = back_src_dev[:, 0]
    back_row, back_col = neighbour_steps(source_owner, n_atmos, n_ocean)
    nearby = extended(response[None, None], (("atm", 0), ("ocn", 1)), 1)
    fetched = nearby.reshape(9 * ocean_count, fields, cells)[
        (back_row * 3 + back_col) * ocean_count + back_src_tile
    ]
    back_part = jnp.einsum("bfi,bij->bfj", fetched, back_blocks, preferred_element_type=jnp.float32)
    atm_import = tile_sums(back_dst_tile, back_part, atmos_count).reshape(
        atmos_count, fields, cells
    )
    return (ocean_import, atm_import)


def solution(mesh):
    in_specs = (
        P(("atm", "ocn"), None, None),
        P(("atm", "ocn"), None, None),
        P(("atm", "ocn")),
        P(("atm", "ocn"), None),
        P(("atm", "ocn")),
        P(("atm", "ocn"), None, None),
        P(("atm", "ocn"), None),
        P(("atm", "ocn"), None, None),
        P(("atm", "ocn"), None),
        P(("atm", "ocn")),
        P(("atm", "ocn")),
    )
    out_specs = (P(("atm", "ocn"), None, None), P(("atm", "ocn"), None, None))
    return jax.shard_map(shards, mesh=mesh, in_specs=in_specs, out_specs=out_specs, check_vma=False)
```

profile of v0, /device:TPU:1, one launch (start us, length us, event | category | flops | bytes accessed | tf_op | source)
XLA Modules:
  0.0 154.6 jit_solution(17515959665222934419)
XLA Ops:
  0.6 0.0 copy-start
  0.7 0.8 fusion.30
  1.4 0.7 fusion.18
  2.1 0.2 convert_reduce_fusion
  2.3 0.7 compare_select_fusion
  3.0 0.7 compare_select_fusion.6
  3.7 0.7 compare_select_fusion.5
  4.5 1.9 %gather_fusion = bf16[192,24,128]{2,1,0:T(8,128)(2,1)} fusion(bf16[128,24,128]{2,1,0:T(8,128)(2,1)S(1)} %copy-done, s32[1024]{0:T(1024)S(1)} %get-tuple-element.17), kind=kCustom, calls=%fused_computation | custom fusion | bytes 2360064 | tf_op jit(solution)/shard_map/gather | solution.py:69
  6.3 4.9 %fusion.39 = f32[192,24,128]{2,1,0:T(8,128)S(1)} fusion(bf16[192,24,128]{2,1,0:T(8,128)(2,1)} %gather_fusion, bf16[192,128,128]{2,1,0:T(8,128)(2,1)} %param.12), kind=kOutput, calls=%fused_computation.108 | convolution fusion | flops 150994944 | bytes 9830400 | tf_op jit(solution)/shard_map/bfi,bij->bfj/dot_general | solution.py:70
  11.2 2.7 %broadcast_in_dim.47 = f32[432,24,128]{2,1,0:T(8,128)} broadcast(f32[]{:T(128)} %constant.98.clone.1), dimensions={} | broadcast | bytes 5308420 | tf_op jit(solution)/shard_map/broadcast_in_dim | solution.py:72
  13.9 23.1 %scatter_fusion = f32[432,24,128]{2,1,0:T(8,128)} fusion(f32[432,24,128]{2,1,0:T(8,128)} %broadcast_in_dim.47, s32[192]{0:T(256)S(1)} %bitcast.58, f32[192,24,128]{2,1,0:T(8,128)S(1)} %fusion.39), kind=kCustom, calls=%fused_computation.3 | custom fusion | bytes 7078656 | tf_op jit(solution)/shard_map/scatter | solution.py:72
  37.0 2.4 %fusion.36 = (f32[144,24,128]{2,1,0:T(8,128)S(1)}, f32[144,24,128]{2,1,0:T(8,128)S(1)}) fusion(f32[432,24,128]{2,1,0:T(8,128)} %scatter_fusion), kind=kLoop, calls=%fused_computation.105 | loop fusion | bytes 7077888 | tf_op jit(solution)/shard_map/slice | solution.py:14
  39.4 2.2 %collective-permute-start.4 = (f32[1,3,48,24,128]{4,3,2,1,0:T(8,128)S(1)}, f32[1,3,48,24,128]{4,3,2,1,0:T(8,128)S(1)}, u32[]{:S(2)}, u32[]{:S(2)}) collective-permute-start(f32[1,3,48,24,128]{4,3,2,1,0:T(8,128)S(1)} %bitcast.54), channel_id=1, source_target_pairs={{0,8},{8,16},{16,24},{24,32},{32,40},{40,48},{48,56},{56,64},{64,7... | collective-permute-start | bytes 5308424 | tf_op jit(solution)/shard_map/ppermute | solution.py:13
  41.6 5.0 %collective-permute-start.5 = (f32[1,3,48,24,128]{4,3,2,1,0:T(8,128)S(1)}, f32[1,3,48,24,128]{4,3,2,1,0:T(8,128)S(1)}, u32[]{:S(2)}, u32[]{:S(2)}) collective-permute-start(f32[1,3,48,24,128]{4,3,2,1,0:T(8,128)S(1)} %bitcast.53), channel_id=1, source_target_pairs={{8,0},{16,8},{24,16},{32,24},{40,32},{48,40},{56,48},{64,56},{72,6... | collective-permute-start | bytes 5308424 | tf_op jit(solution)/shard_map/ppermute | solution.py:16
  46.6 38.2 %collective-permute-done.4 = f32[1,3,48,24,128]{4,3,2,1,0:T(8,128)S(1)} collective-permute-done((f32[1,3,48,24,128]{4,3,2,1,0:T(8,128)S(1)}, f32[1,3,48,24,128]{4,3,2,1,0:T(8,128)S(1)}, u32[]{:S(2)}, u32[]{:S(2)}) %collective-permute-start.4) | collective-permute-done | bytes 1769504 | tf_op jit(solution)/shard_map/ppermute | solution.py:13
  84.9 0.0 copy-start.5
  84.9 3.1 %pad_maximum_fusion.3 = (f32[5,1,48,24,128]{4,3,2,1,0:T(8,128)}, f32[5,1,48,24,128]{4,3,2,1,0:T(8,128)}) fusion(f32[1,3,48,24,128]{4,3,2,1,0:T(8,128)S(1)} %collective-permute-done.5, f32[3,3,48,24,128]{4,3,2,1,0:T(8,128)S(1)} %bitcast.49, f32[1,3,48,24,128]{4,3,2,1,0:T(8,128)S(1)} %collective-permute-done.4), kind=kLoop, calls=%fused_computation.11 | loop fusion | flops 2949120 | bytes 14745600 | tf_op jit(solution)/shard_map/slice | solution.py:14
  88.0 2.3 %collective-permute-start.6 = (f32[5,1,48,24,128]{4,3,2,1,0:T(8,128)}, f32[5,1,48,24,128]{4,3,2,1,0:T(8,128)}, u32[]{:S(2)}, u32[]{:S(2)}) collective-permute-start(f32[5,1,48,24,128]{4,3,2,1,0:T(8,128)} %get-tuple-element.8), channel_id=1, source_target_pairs={{0,1},{1,2},{2,3},{3,4},{4,5},{5,6},{6,7},{7,0},{8,9},{9,10},{10,1... | collective-permute-start | bytes 8847368 | tf_op jit(solution)/shard_map/ppermute | solution.py:13
  90.3 1.4 scatter_custom_fusion
  91.6 0.1 fusion.38
  91.7 0.1 slice.59
  91.8 0.1 slice.61
  91.9 4.9 %collective-permute-start.1 = (s32[1,3,48]{2,1,0:T(4,128)S(1)}, s32[1,3,48]{2,1,0:T(4,128)S(1)}, u32[]{:S(2)}, u32[]{:S(2)}) collective-permute-start(s32[1,3,48]{2,1,0:T(4,128)S(1)} %slice.61), channel_id=1, source_target_pairs={{8,0},{16,8},{24,16},{32,24},{40,32},{48,40},{56,48},{64,56},{72,6... | collective-permute-start | bytes 1736 | tf_op jit(solution)/shard_map/ppermute | solution.py:16
  96.7 0.1 reshape.126
  96.8 0.8 collective-permute-done
  97.7 2.8 %collective-permute-start.2 = (s32[5,1,48]{2,1,0:T(1,128)S(1)}, s32[5,1,48]{2,1,0:T(1,128)S(1)}, u32[]{:S(2)}, u32[]{:S(2)}) collective-permute-start(s32[5,1,48]{2,1,0:T(1,128)S(1)} %get-tuple-element.12), channel_id=1, source_target_pairs={{0,1},{1,2},{2,3},{3,4},{4,5},{5,6},{6,7},{7,0},{8,9},{9,10},{10,1... | collective-permute-start | bytes 2888 | tf_op jit(solution)/shard_map/ppermute | solution.py:13
  100.5 0.2 collective-permute-start.3
  100.7 22.0 %collective-permute-done.2 = s32[5,1,48]{2,1,0:T(1,128)S(1)} collective-permute-done((s32[5,1,48]{2,1,0:T(1,128)S(1)}, s32[5,1,48]{2,1,0:T(1,128)S(1)}, u32[]{:S(2)}, u32[]{:S(2)}) %collective-permute-start.2) | collective-permute-done | bytes 992 | tf_op jit(solution)/shard_map/ppermute | solution.py:13
  122.7 2.5 %collective-permute-done.3 = s32[5,1,48]{2,1,0:T(1,128)S(1)} collective-permute-done((s32[5,1,48]{2,1,0:T(1,128)S(1)}, s32[5,1,48]{2,1,0:T(1,128)S(1)}, u32[]{:S(2)}, u32[]{:S(2)}) %collective-permute-start.3) | collective-permute-done | bytes 992 | tf_op jit(solution)/shard_map/ppermute | solution.py:16
  125.2 0.1 slice.64
  125.3 0.1 eq.118
  125.4 5.9 %pad_maximum_fusion = f32[5,5,48,24,128]{4,3,2,1,0:T(8,128)S(1)} fusion(f32[5,1,48,24,128]{4,3,2,1,0:T(8,128)} %collective-permute-done.7, f32[1,3,48,24,128]{4,3,2,1,0:T(8,128)} %copy-done.3, f32[3,3,48,24,128]{4,3,2,1,0:T(8,128)} %bitcast.48, f32[1,3,48,24,128]{4,3,2,1,0:T(8,128)S(1)} %collective-permute-done.4, ...), kind=kLoop, calls=%fused_computation.4 | loop fusion | flops 14745600 | bytes 29491200 | tf_op jit(solution)/shard_map/concatenate | solution.py:17
  131.4 0.4 slice.71
  131.8 2.2 %fusion = f32[8,24,128]{2,0,1:T(8,128)S(1)} fusion(s32[432]{0:T(512)S(1)} %eq.118, f32[54,8,24,128]{3,2,1,0:T(8,128)S(1)} %bitcast.50), kind=kOutput, calls=%fused_computation.6 | convolution fusion | flops 127405440 | bytes 5408448 | tf_op jit(solution)/shard_map/dot_general | solution.py:31
  134.0 0.1 collective-permute-start.8
  134.1 5.1 %collective-permute-start.9 = (bf16[1,1,8,24,128]{4,2,3,1,0:T(8,128)(2,1)S(1)}, bf16[1,1,8,24,128]{4,2,3,1,0:T(8,128)(2,1)S(1)}, u32[]{:S(2)}, u32[]{:S(2)}) collective-permute-start(bf16[1,1,8,24,128]{4,2,3,1,0:T(8,128)(2,1)S(1)} %fusion.12), channel_id=1, source_target_pairs={{8,0},{16,8},{24,16},{32,24},{40,32},{48,40},{56,48},{64,56},{72,6... | collective-permute-start | bytes 147464 | tf_op jit(solution)/shard_map/ppermute | solution.py:16
  139.2 1.2 collective-permute-done.8
  140.4 1.1 collective-permute-start.10
  141.5 0.2 collective-permute-start.11
  141.7 0.7 copy.26
  142.3 1.3 collective-permute-done.10
  143.6 2.8 %collective-permute-done.11 = bf16[3,1,8,24,128]{4,2,3,1,0:T(8,128)(2,1)S(1)} collective-permute-done((bf16[3,1,8,24,128]{4,2,3,1,0:T(8,128)(2,1)S(1)}, bf16[3,1,8,24,128]{4,2,3,1,0:T(8,128)(2,1)S(1)}, u32[]{:S(2)}, u32[]{:S(2)}) %collective-permute-start.11) | collective-permute-done | bytes 147488 | tf_op jit(solution)/shard_map/ppermute | solution.py:16
  146.4 0.1 pad_maximum_fusion.4
  146.4 0.1 copy.24
  146.5 0.9 gather_fusion.1
  147.4 3.8 %fusion.40 = f32[192,24,128]{2,1,0:T(8,128)S(1)} fusion(bf16[192,24,128]{2,1,0:T(8,128)(2,1)S(1)} %gather_fusion.1, bf16[192,128,128]{2,1,0:T(8,128)(2,1)} %param.18), kind=kOutput, calls=%fused_computation.109 | convolution fusion | flops 150994944 | bytes 9830400 | tf_op jit(solution)/shard_map/bfi,bij->bfj/dot_general | solution.py:91
  151.2 1.4 fusion.3
  152.6 2.1 %copy.27 = f32[128,24,128]{2,1,0:T(8,128)} copy(f32[128,24,128]{2,0,1:T(8,128)S(1)} %fusion.3) | data formatting | bytes 3145728
  (28 shorter events, 0.1 us)
Async XLA Ops:
  0.6 3.8 %copy-start = (bf16[128,24,128]{2,1,0:T(8,128)(2,1)S(1)}, bf16[128,24,128]{2,1,0:T(8,128)(2,1)}, u32[]{:S(2)}) copy-start(bf16[128,24,128]{2,1,0:T(8,128)(2,1)} %param.11) | copy-start | bytes 2359300
  37.0 47.8 %copy-start.2 = (f32[432,24,128]{2,1,0:T(8,128)S(1)}, f32[432,24,128]{2,1,0:T(8,128)}, u32[]{:S(2)}) copy-start(f32[432,24,128]{2,1,0:T(8,128)} %scatter_fusion) | copy-start | bytes 15925252
  39.4 45.4 %collective-permute-start.4 = (f32[1,3,48,24,128]{4,3,2,1,0:T(8,128)S(1)}, f32[1,3,48,24,128]{4,3,2,1,0:T(8,128)S(1)}, u32[]{:S(2)}, u32[]{:S(2)}) collective-permute-start(f32[1,3,48,24,128]{4,3,2,1,0:T(8,128)S(1)} %bitcast.54), channel_id=1, source_target_pairs={{0,8},{8,16},{16,24},{24,32},{32,40},{40,48},{48,56},{56,64},{64,7... | collective-permute-start | bytes 5308424 | tf_op jit(solution)/shard_map/ppermute | solution.py:13
  41.6 43.3 %collective-permute-start.5 = (f32[1,3,48,24,128]{4,3,2,1,0:T(8,128)S(1)}, f32[1,3,48,24,128]{4,3,2,1,0:T(8,128)S(1)}, u32[]{:S(2)}, u32[]{:S(2)}) collective-permute-start(f32[1,3,48,24,128]{4,3,2,1,0:T(8,128)S(1)} %bitcast.53), channel_id=1, source_target_pairs={{8,0},{16,8},{24,16},{32,24},{40,32},{48,40},{56,48},{64,56},{72,6... | collective-permute-start | bytes 5308424 | tf_op jit(solution)/shard_map/ppermute | solution.py:16
  84.9 3.1 %copy-start.3 = (f32[1,3,48,24,128]{4,3,2,1,0:T(8,128)}, f32[1,3,48,24,128]{4,3,2,1,0:T(8,128)S(1)}, u32[]{:S(2)}) copy-start(f32[1,3,48,24,128]{4,3,2,1,0:T(8,128)S(1)} %collective-permute-done.5) | copy-start | bytes 5308420
  84.9 15.8 %copy-start.5 = (s32[8,128]{1,0:T(8,128)S(1)}, s32[8,128]{1,0:T(8,128)}, u32[]{:S(2)}) copy-start(s32[8,128]{1,0:T(8,128)} %param.17) | copy-start | bytes 12292
  88.0 37.4 %collective-permute-start.6 = (f32[5,1,48,24,128]{4,3,2,1,0:T(8,128)}, f32[5,1,48,24,128]{4,3,2,1,0:T(8,128)}, u32[]{:S(2)}, u32[]{:S(2)}) collective-permute-start(f32[5,1,48,24,128]{4,3,2,1,0:T(8,128)} %get-tuple-element.8), channel_id=1, source_target_pairs={{0,1},{1,2},{2,3},{3,4},{4,5},{5,6},{6,7},{7,0},{8,9},{9,10},{10,1... | collective-permute-start | bytes 8847368 | tf_op jit(solution)/shard_map/ppermute | solution.py:13
  90.3 35.2 %collective-permute-start.7 = (f32[5,1,48,24,128]{4,3,2,1,0:T(8,128)}, f32[5,1,48,24,128]{4,3,2,1,0:T(8,128)}, u32[]{:S(2)}, u32[]{:S(2)}) collective-permute-start(f32[5,1,48,24,128]{4,3,2,1,0:T(8,128)} %get-tuple-element.9), channel_id=1, source_target_pairs={{1,0},{2,1},{3,2},{4,3},{5,4},{6,5},{7,6},{0,7},{9,8},{10,9},{11,1... | collective-permute-start | bytes 8847368 | tf_op jit(solution)/shard_map/ppermute | solution.py:16
  91.8 5.8 %collective-permute-start = (s32[1,3,48]{2,1,0:T(4,128)S(1)}, s32[1,3,48]{2,1,0:T(4,128)S(1)}, u32[]{:S(2)}, u32[]{:S(2)}) collective-permute-start(s32[1,3,48]{2,1,0:T(4,128)S(1)} %slice.59), channel_id=1, source_target_pairs={{0,8},{8,16},{16,24},{24,32},{32,40},{40,48},{48,56},{56,64},{64,7... | collective-permute-start | bytes 1736 | tf_op jit(solution)/shard_map/ppermute | solution.py:13
  91.9 5.8 %collective-permute-start.1 = (s32[1,3,48]{2,1,0:T(4,128)S(1)}, s32[1,3,48]{2,1,0:T(4,128)S(1)}, u32[]{:S(2)}, u32[]{:S(2)}) collective-permute-start(s32[1,3,48]{2,1,0:T(4,128)S(1)} %slice.61), channel_id=1, source_target_pairs={{8,0},{16,8},{24,16},{32,24},{40,32},{48,40},{56,48},{64,56},{72,6... | collective-permute-start | bytes 1736 | tf_op jit(solution)/shard_map/ppermute | solution.py:16
  97.7 25.0 %collective-permute-start.2 = (s32[5,1,48]{2,1,0:T(1,128)S(1)}, s32[5,1,48]{2,1,0:T(1,128)S(1)}, u32[]{:S(2)}, u32[]{:S(2)}) collective-permute-start(s32[5,1,48]{2,1,0:T(1,128)S(1)} %get-tuple-element.12), channel_id=1, source_target_pairs={{0,1},{1,2},{2,3},{3,4},{4,5},{5,6},{6,7},{7,0},{8,9},{9,10},{10,1... | collective-permute-start | bytes 2888 | tf_op jit(solution)/shard_map/ppermute | solution.py:13
  100.5 24.7 %collective-permute-start.3 = (s32[5,1,48]{2,1,0:T(1,128)S(1)}, s32[5,1,48]{2,1,0:T(1,128)S(1)}, u32[]{:S(2)}, u32[]{:S(2)}) collective-permute-start(s32[5,1,48]{2,1,0:T(1,128)S(1)} %get-tuple-element.13), channel_id=1, source_target_pairs={{1,0},{2,1},{3,2},{4,3},{5,4},{6,5},{7,6},{0,7},{9,8},{10,9},{11,1... | collective-permute-start | bytes 2888 | tf_op jit(solution)/shard_map/ppermute | solution.py:16
  131.8 2.2 %copy-start.4 = (f32[8,24,128]{2,1,0:T(8,128)S(1)}, f32[8,24,128]{2,1,0:T(8,128)}, u32[]{:S(2)}) copy-start(f32[8,24,128]{2,1,0:T(8,128)} %param.16) | copy-start | bytes 294916
  134.0 6.4 %collective-permute-start.8 = (bf16[1,1,8,24,128]{4,2,3,1,0:T(8,128)(2,1)S(1)}, bf16[1,1,8,24,128]{4,2,3,1,0:T(8,128)(2,1)S(1)}, u32[]{:S(2)}, u32[]{:S(2)}) collective-permute-start(bf16[1,1,8,24,128]{4,2,3,1,0:T(8,128)(2,1)S(1)} %fusion.12), channel_id=1, source_target_pairs={{0,8},{8,16},{16,24},{24,32},{32,40},{40,48},{48,56},{56,64},{64,7... | collective-permute-start | bytes 147464 | tf_op jit(solution)/shard_map/ppermute | solution.py:13
  134.1 6.3 %collective-permute-start.9 = (bf16[1,1,8,24,128]{4,2,3,1,0:T(8,128)(2,1)S(1)}, bf16[1,1,8,24,128]{4,2,3,1,0:T(8,128)(2,1)S(1)}, u32[]{:S(2)}, u32[]{:S(2)}) collective-permute-start(bf16[1,1,8,24,128]{4,2,3,1,0:T(8,128)(2,1)S(1)} %fusion.12), channel_id=1, source_target_pairs={{8,0},{16,8},{24,16},{32,24},{40,32},{48,40},{56,48},{64,56},{72,6... | collective-permute-start | bytes 147464 | tf_op jit(solution)/shard_map/ppermute | solution.py:16
  140.4 3.2 %collective-permute-start.10 = (bf16[3,1,8,24,128]{4,2,3,1,0:T(8,128)(2,1)S(1)}, bf16[3,1,8,24,128]{4,2,3,1,0:T(8,128)(2,1)S(1)}, u32[]{:S(2)}, u32[]{:S(2)}) collective-permute-start(bf16[3,1,8,24,128]{4,2,3,1,0:T(8,128)(2,1)S(1)} %pad_maximum_fusion.5), channel_id=1, source_target_pairs={{0,1},{1,2},{2,3},{3,4},{4,5},{5,6},{6,7},{7,0},{8,9},{9,10},{10,1... | collective-permute-start | bytes 442376 | tf_op jit(solution)/shard_map/ppermute | solution.py:13
  141.5 4.9 %collective-permute-start.11 = (bf16[3,1,8,24,128]{4,2,3,1,0:T(8,128)(2,1)S(1)}, bf16[3,1,8,24,128]{4,2,3,1,0:T(8,128)(2,1)S(1)}, u32[]{:S(2)}, u32[]{:S(2)}) collective-permute-start(bf16[3,1,8,24,128]{4,2,3,1,0:T(8,128)(2,1)S(1)} %pad_maximum_fusion.5), channel_id=1, source_target_pairs={{1,0},{2,1},{3,2},{4,3},{5,4},{6,5},{7,6},{0,7},{9,8},{10,9},{11,1... | collective-permute-start | bytes 442376 | tf_op jit(solution)/shard_map/ppermute | solution.py:16
  147.4 3.8 %copy-start.6 = (s32[192]{0:T(256)S(1)}, s32[192]{0:T(256)}, u32[]{:S(2)}) copy-start(s32[192]{0:T(256)} %param.21) | copy-start | bytes 2308
  151.2 3.5 %copy-start.1 = (bf16[128,24,128]{2,1,0:T(8,128)(2,1)S(1)}, bf16[128,24,128]{2,1,0:T(8,128)(2,1)}, u32[]{:S(2)}) copy-start(bf16[128,24,128]{2,1,0:T(8,128)(2,1)} %param.11) | copy-start | bytes 2359300
where the time goes:
time: 156 us; the launch traced here: 155 us
  waiting for transfers between devices  68.8 us (44%)
  local copies, waits for them, and re-layouts  36.1 us (23%)
  starting transfers between devices  23.8 us (15%)
  other arithmetic  12.9 us (8%)
  matrix products  12.2 us (8%)
    ppermute x6, waiting for transfers between devices, extended(): lax.ppermute(lax.slice_in_dim(block, block.shape[dim] - width, None, axis...  63.6 us
    scatter x1, local copies, waits for them, and re-layouts, shards(): jnp.zeros((9 * slots, fields, cells), jnp.float32).at[place].set(fwd_part)  23.1 us
    ppermute x6, starting transfers between devices, extended(): lax.ppermute(lax.slice_in_dim(block, 0, width, axis=dim), axis, backward)  15.3 us
    ppermute x6, starting transfers between devices, extended(): lax.ppermute(lax.slice_in_dim(block, block.shape[dim] - width, None, axis...  8.47 us
    concatenate x4, other arithmetic, extended(): block = jnp.concatenate([low, block, high], axis=dim)  6.02 us
    ppermute x6, waiting for transfers between devices, extended(): lax.ppermute(lax.slice_in_dim(block, 0, width, axis=dim), axis, backward)  5.25 us
    dot_general x1, matrix products, shards(): jnp.einsum('bfi,bij->bfj', sources, fwd_blocks, preferred_element_type=jn...  4.9 us
    dot_general x1, matrix products, shards(): jnp.einsum('bfi,bij->bfj', fetched, back_blocks, preferred_element_type=j...  3.78 us
  transfers between devices with their start and end apart: 12, of which 7 were waited for; matrix products, arithmetic and copies ran while one was open for 2% of the time, Pallas kernels for 0%

commit v1 on v0

v1 whole, which is shorter than its diff:
```python
import functools

import jax
import jax.numpy as jnp
from jax import lax
from jax.experimental import pallas as pl
from jax.experimental.pallas import tpu as pltpu
from jax.sharding import PartitionSpec as P

MESH = pl.DeviceIdType.MESH
I32 = jnp.int32
F32 = jnp.float32
HALVES = 2
LEVELS = 32766.0
ORDER = (0, 2, 6, 8, 1, 7, 3, 5)
SELF = 4


def steps(n):
    return n // 3 - 1, n % 3 - 1


def neighbour_keys(dev, tile, here_row, here_col, n_row, n_col, tiles):
    shift = n_col.bit_length() - 1
    rel_row = ((dev >> shift) - here_row) & (n_row - 1)
    rel_col = ((dev & (n_col - 1)) - here_col) & (n_col - 1)
    row_step = jnp.where(rel_row == n_row - 1, 0, jnp.where(rel_row == 0, 1, 2))
    col_step = jnp.where(rel_col == n_col - 1, 0, jnp.where(rel_col == 0, 1, 2))
    return (row_step * 3 + col_step) * tiles + tile


def sorted_order(key, src, tiles):
    count = key.shape[1]
    group = count // HALVES
    lane = lax.broadcasted_iota(I32, (1, count), 1)
    half = jnp.zeros_like(lane)
    for h in range(1, HALVES):
        half = half + (lane >= h * group).astype(I32)
    wide_key = half * 128 + key
    rank_row = wide_key * 256 + lane
    eye = lax.broadcasted_iota(I32, (count, count), 0) == lax.broadcasted_iota(
        I32, (count, count), 1
    )

    def column(row):
        return jnp.sum(jnp.where(eye, row, 0), axis=1, keepdims=True)

    rank_col = column(rank_row)
    src_col = column(src)
    place = jnp.sum((rank_row < rank_col).astype(I32), axis=1, keepdims=True)
    lanes = lax.broadcasted_iota(I32, (count, 256), 1)
    hit = place == lanes
    local = (rank_col & 255) - (rank_col >> 15) * group
    key_col = rank_col >> 8

    def arranged(col):
        return jnp.sum(jnp.where(hit, col, 0), axis=0, keepdims=True)

    rows = [arranged(local), arranged(src_col), arranged(key_col)]
    for h in range(HALVES):
        slot = lanes + h * 128
        inside = (key_col == slot) & (lanes < 128)
        upto = jnp.sum((key_col <= slot).astype(I32), axis=0, keepdims=True)
        some = jnp.sum(inside.astype(I32), axis=0, keepdims=True)
        rows.append(jnp.where(some > 0, upto - 1, -1))
    return rows


def exchange(
    n_row,
    n_col,
    src_hbm,
    dev_hbm,
    tile_hbm,
    atm_hbm,
    w_hbm,
    state_hbm,
    mask_hbm,
    import_ref,
    near_ref,
    src_ref,
    dev_ref,
    tile_ref,
    state_ref,
    mask_ref,
    small_sem,
    atm_v,
    *scratch,
):
    w_v = scratch[:HALVES]
    (
        sums,
        prep_v,
        prep_s,
        q_out,
        scale_out,
        q_in,
        scale_in,
        atm_sem,
        w_sem,
        prep_sem,
        send_sem,
        recv_sem,
        scale_send_sem,
        scale_recv_sem,
        resp_send_sem,
        resp_recv_sem,
    ) = scratch[HALVES:]
    count = dev_ref.shape[1]
    group = count // HALVES
    tiles, fields, cells = state_ref.shape
    row = lax.axis_index("atm")
    col = lax.axis_index("ocn")

    def device(n):
        dr, dc = steps(n)
        return (lax.rem(row + dr + n_row, n_row), lax.rem(col + dc + n_col, n_col))

    barrier = pltpu.get_barrier_semaphore()
    for n in ORDER:
        pl.semaphore_signal(barrier, inc=1, device_id=device(n), device_id_type=MESH)

    small_copies = [
        pltpu.make_async_copy(source, target, small_sem.at[i])
        for i, (source, target) in enumerate(
            (
                (src_hbm, src_ref),
                (dev_hbm, dev_ref),
                (tile_hbm, tile_ref),
                (state_hbm, state_ref),
                (mask_hbm, mask_ref),
            )
        )
    ]
    for copy in small_copies:
        copy.start()
    atm_copy = pltpu.make_async_copy(atm_hbm, atm_v, atm_sem)
    atm_copy.start()
    w_copies = []
    for h in range(HALVES):
        copy = pltpu.make_async_copy(
            w_hbm.at[pl.ds(h * group, group)], w_v[h], w_sem.at[h]
        )
        copy.start()
        w_copies.append(copy)

    for copy in small_copies[:3]:
        copy.wait()
    key = neighbour_keys(dev_ref[...], tile_ref[...], row, col, n_row, n_col, tiles)
    rows = sorted_order(key, src_ref[...], tiles)
    for i, values in enumerate(rows):
        prep_v[i : i + 1, :] = values
    prep_copy = pltpu.make_async_copy(prep_v, prep_s, prep_sem)
    prep_copy.start()
    prep_copy.wait()
    atm_copy.wait()

    for h in range(HALVES):
        w_copies[h].wait()

        def one(i, total, h=h):
            k = h * group + i
            before = prep_s[2, jnp.maximum(k - 1, 0)]
            keep = jnp.where((prep_s[2, k] == before) & (i > 0), 1.0, 0.0).astype(F32)
            product = jnp.dot(
                atm_v[prep_s[1, k]], w_v[h][prep_s[0, k]], preferred_element_type=F32
            )
            total = total * keep + product
            sums[k] = total
            return total

        lax.fori_loop(0, group, one, jnp.zeros((fields, cells), F32), unroll=8)

    def slot_sum(slot):
        total = None
        for h in range(HALVES):
            last = prep_s[3 + h, slot]
            part = sums[jnp.maximum(last, 0)] * jnp.where(last >= 0, 1.0, 0.0).astype(F32)
            total = part if total is None else total + part
        return total

    pl.semaphore_wait(barrier, 8)
    copies = []
    for n in ORDER:
        for t in range(tiles):
            total = slot_sum(n * tiles + t)
            top = jnp.max(jnp.abs(total), axis=0, keepdims=True)
            q_out[n, t] = jnp.round(total * (LEVELS / jnp.maximum(top, 1e-30))).astype(
                jnp.int16
            )
            scale_out[n, t : t + 1] = top * (1.0 / LEVELS)
        for out, land, s_sem, r_sem in (
            (q_out, q_in, send_sem, recv_sem),
            (scale_out, scale_in, scale_send_sem, scale_recv_sem),
        ):
            copy = pltpu.make_async_remote_copy(
                src_ref=out.at[n],
                dst_ref=land.at[8 - n],
                send_sem=s_sem.at[n],
                recv_sem=r_sem.at[8 - n],
                device_id=device(n),
                device_id_type=MESH,
            )
            copy.start()
            copies.append(copy)
    for t in range(tiles):
        import_ref[t] = slot_sum(SELF * tiles + t)
    for copy in small_copies[3:]:
        copy.wait()
    for copy in copies:
        copy.wait()

    for t in range(tiles):
        total = import_ref[t]
        for n in ORDER:
            total = total + q_in[n, t].astype(F32) * scale_in[n, t : t + 1]
        import_ref[t] = total
        wet = mask_ref[t : t + 1].astype(F32)
        near_ref[SELF, t] = (wet * jnp.tanh(state_ref[t] + total)).astype(jnp.bfloat16)

    copies = []
    for n in ORDER:
        copy = pltpu.make_async_remote_copy(
            src_ref=near_ref.at[SELF],
            dst_ref=near_ref.at[8 - n],
            send_sem=resp_send_sem.at[n],
            recv_sem=resp_recv_sem.at[8 - n],
            device_id=device(n),
            device_id_type=MESH,
        )
        copy.start()
        copies.append(copy)
    for copy in copies:
        copy.wait()


def backward(n_row, n_col, dev_ref, tile_ref, dst_ref, near_ref, import_ref, w_ref, imported_ref, out_ref):
    count = dst_ref.shape[0]
    atmos, fields, cells = out_ref.shape
    tiles = near_ref.shape[0] // 9
    row = lax.axis_index("atm")
    col = lax.axis_index("ocn")
    imported_ref[...] = import_ref[...]

    def clear(t, _):
        out_ref[t] = jnp.zeros((fields, cells), F32)
        return 0

    lax.fori_loop(0, atmos, clear, 0, unroll=8)

    def one(b, _):
        slot = neighbour_keys(dev_ref[b], tile_ref[b], row, col, n_row, n_col, tiles)
        product = jnp.dot(near_ref[slot], w_ref[b], preferred_element_type=F32)
        dst = dst_ref[b]
        out_ref[dst] = out_ref[dst] + product
        return 0

    lax.fori_loop(0, count, one, 0, unroll=8)


def shards(
    atm_fields,
    fwd_blocks,
    fwd_src_tile,
    fwd_dst_dev,
    fwd_dst_tile,
    ocean_state,
    wet_mask,
    back_blocks,
    back_src_dev,
    back_src_tile,
    back_dst_tile,
):
    n_row = lax.axis_size("atm")
    n_col = lax.axis_size("ocn")
    blocks, cells, _ = fwd_blocks.shape
    group = blocks // HALVES
    atmos, fields, _ = atm_fields.shape
    tiles = ocean_state.shape[0]
    vmem = pl.BlockSpec(memory_space=pltpu.VMEM)
    smem = pl.BlockSpec(memory_space=pltpu.SMEM)
    hbm = pl.BlockSpec(memory_space=pltpu.HBM)
    ocean_import, near = pl.pallas_call(
        functools.partial(exchange, n_row, n_col),
        out_shape=(
            jax.ShapeDtypeStruct((tiles, fields, cells), F32),
            jax.ShapeDtypeStruct((9, tiles, fields, cells), jnp.bfloat16),
        ),
        in_specs=[hbm] * 7,
        out_specs=(vmem, vmem),
        scratch_shapes=[
            pltpu.VMEM((1, blocks), I32),
            pltpu.VMEM((1, blocks), I32),
            pltpu.VMEM((1, blocks), I32),
            pltpu.VMEM((tiles, fields, cells), F32),
            pltpu.VMEM((tiles, cells), I32),
            pltpu.SemaphoreType.DMA((5,)),
            pltpu.VMEM((atmos, fields, cells), jnp.bfloat16),
            *[pltpu.VMEM((group, cells, cells), jnp.bfloat16)] * HALVES,
            pltpu.VMEM((blocks, fields, cells), F32),
            pltpu.VMEM((8, 256), I32),
            pltpu.SMEM((8, 256), I32),
            pltpu.VMEM((9, tiles, fields, cells), jnp.int16),
            pltpu.VMEM((9, tiles, cells), F32),
            pltpu.VMEM((9, tiles, fields, cells), jnp.int16),
            pltpu.VMEM((9, tiles, cells), F32),
            pltpu.SemaphoreType.DMA,
            pltpu.SemaphoreType.DMA((HALVES,)),
            pltpu.SemaphoreType.DMA,
            *[pltpu.SemaphoreType.DMA((9,))] * 6,
        ],
        compiler_params=pltpu.CompilerParams(
            collective_id=0, has_side_effects=True, vmem_limit_bytes=24 * 2**20
        ),
        name="exchange",
    )(
        *[
            pltpu.with_memory_space_constraint(operand, pltpu.HBM)
            for operand in (
                fwd_src_tile.reshape(1, blocks),
                fwd_dst_dev.reshape(1, blocks),
                fwd_dst_tile.reshape(1, blocks),
                atm_fields,
                fwd_blocks,
                ocean_state,
                wet_mask,
            )
        ]
    )
    return pl.pallas_call(
        functools.partial(backward, n_row, n_col),
        out_shape=(
            jax.ShapeDtypeStruct((tiles, fields, cells), F32),
            jax.ShapeDtypeStruct((atmos, fields, cells), F32),
        ),
        in_specs=[smem, smem, smem, vmem, vmem, vmem],
        out_specs=(vmem, vmem),
        compiler_params=pltpu.CompilerParams(vmem_limit_bytes=24 * 2**20),
        name="backward",
    )(
        back_src_dev.reshape(blocks),
        back_src_tile,
        back_dst_tile,
        near.reshape(9 * tiles, fields, cells),
        ocean_import,
        back_blocks,
    )


def solution(mesh):
    both = ("atm", "ocn")
    in_specs = (
        P(both, None, None),
        P(both, None, None),
        P(both),
        P(both, None),
        P(both),
        P(both, None, None),
        P(both, None),
        P(both, None, None),
        P(both, None),
        P(both),
        P(both),
    )
    out_specs = (P(both, None, None), P(both, None, None))
    return jax.shard_map(shards, mesh=mesh, in_specs=in_specs, out_specs=out_specs, check_vma=False)
```

time: 156 us -> 31.1 us (0.20)
  waiting for transfers between devices: 68.8 us -> 0 us
  local copies, waits for them, and re-layouts: 36.1 us -> 0.02 us
  Pallas kernels: 0 us -> 30.3 us
  starting transfers between devices: 23.8 us -> 0 us
  other arithmetic: 12.9 us -> 0 us
  matrix products: 12.2 us -> 0 us
    ppermute x12 -> x0, waiting for transfers between devices: 68.8 us -> none  [the longest x6 63.6 us: extended(): lax.ppermute(lax.slice_in_dim(block, block.shape[dim] - width, None, axis...]
    pallas_call x0 -> x2, Pallas kernels: none -> 30.3 us  [the longest x1 24 us: shards(): pl.pallas_call(functools.partial(exchange, n_row, n_col), out_shape=(jax....]
    scatter x2 -> x0, local copies, waits for them, and re-layouts: 24.4 us -> none  [the longest x1 23.1 us: shards(): jnp.zeros((9 * slots, fields, cells), jnp.float32).at[place].set(fwd_part)]
    ppermute x12 -> x0, starting transfers between devices: 23.8 us -> none  [the longest x6 15.3 us: extended(): lax.ppermute(lax.slice_in_dim(block, 0, width, axis=dim), axis, backward)]
    dot_general x4 -> x0, matrix products: 12.2 us -> none  [the longest x1 4.9 us: shards(): jnp.einsum('bfi,bij->bfj', sources, fwd_blocks, preferred_element_type=jn...]
    concatenate x4 -> x0, other arithmetic: 6.02 us -> none  [extended(): block = jnp.concatenate([low, block, high], axis=dim)]
    slice x7 -> x0, local copies, waits for them, and re-layouts: 3.14 us -> none  [the longest x3 2.48 us: extended(): lax.slice_in_dim(block, block.shape[dim] - width, None, axis=dim)]
    slice x1 -> x0, other arithmetic: 3.08 us -> none  [extended(): lax.slice_in_dim(block, block.shape[dim] - width, None, axis=dim)]
  transfers between devices with their start and end apart: 12 -> 0, of which waited for: 7 -> 0; matrix products, arithmetic and copies ran while one was open for 2% -> 0% of each run, Pallas kernels for 0% -> 0%
where the time goes in v1:
time: 31.1 us; the launch traced here: 31 us
  Pallas kernels  30.3 us (97%)
  between operations  0.71 us (2%)
    pallas_call x1, Pallas kernels, shards(): pl.pallas_call(functools.partial(exchange, n_row, n_col), out_shape=(jax....  24 us
    pallas_call x1, Pallas kernels, shards(): pl.pallas_call(functools.partial(backward, n_row, n_col), out_shape=(jax....  6.36 us

profile of v1, /device:TPU:1, one launch (start us, length us, event | category | flops | bytes accessed | tf_op | source)
XLA Modules:
  0.0 31.0 jit_solution(6201018330039710248)
XLA Ops:
  0.6 0.0 copy-start.3
  0.6 0.0 copy-start.2
  0.7 0.0 copy-start.1
  0.7 0.0 copy-start
  0.7 24.0 %exchange.1 = (f32[8,24,128]{2,1,0:T(8,128)S(1)}, bf16[9,8,24,128]{3,2,1,0:T(8,128)(2,1)S(1)}) custom-call(s32[1,192]{1,0:T(1,128)} %bitcast.7, s32[1,192]{1,0:T(1,128)} %bitcast.8, s32[1,192]{1,0:T(1,128)} %bitcast.9, bf16[128,24,128]{2,1,0:T(8,128)(2,1)} %atm_hbm.1, bf16[192,128,128]{2,1,0:T(8,128)(2,1)} %w_hbm.1, f32[8,24,128]{2,1,0:T(8,128)} %state_hbm.1, ...), custom_call_target="tpu_custom_call" | custom-call | tf_op jit(solution)/shard_map/exchange/pallas_call | solution.py:283
  24.6 0.0 copy-done.3
  24.6 0.0 copy-done.2
  24.7 0.0 copy-done.1
  24.7 0.0 copy-done
  24.7 6.4 %backward.1 = (f32[8,24,128]{2,1,0:T(8,128)}, f32[128,24,128]{2,1,0:T(8,128)}) custom-call(s32[192]{0:T(256)S(1)} %bitcast.6, s32[192]{0:T(256)S(1)} %copy-done.2, s32[192]{0:T(256)S(1)} %copy-done.3, bf16[72,24,128]{2,1,0:T(8,128)(2,1)S(1)} %bitcast.5, f32[8,24,128]{2,1,0:T(8,128)S(1)} %get-tuple-element.5.import_ref, bf16[192,128,128]{2,1,0:T(8,128)(2,1)S(1)} %copy-done), custom_call_target="tpu_custom_call" | custom-call | tf_op jit(solution)/shard_map/backward/pallas_call | solution.py:330
Async XLA Ops:
  0.6 24.0 %copy-start.3 = (s32[192]{0:T(256)S(1)}, s32[192]{0:T(256)}, u32[]{:S(2)}) copy-start(s32[192]{0:T(256)} %dst_ref.1) | copy-start | bytes 2308
  0.6 24.0 %copy-start.2 = (s32[192]{0:T(256)S(1)}, s32[192]{0:T(256)}, u32[]{:S(2)}) copy-start(s32[192]{0:T(256)} %tile_ref.1) | copy-start | bytes 2308
  0.7 24.0 %copy-start.1 = (s32[192,1]{0,1:T(1,128)S(1)}, s32[192,1]{0,1:T(1,128)}, u32[]{:S(2)}) copy-start(s32[192,1]{0,1:T(1,128)} %param.19) | copy-start | bytes 2308
  0.7 24.0 %copy-start = (bf16[192,128,128]{2,1,0:T(8,128)(2,1)S(1)}, bf16[192,128,128]{2,1,0:T(8,128)(2,1)}, u32[]{:S(2)}) copy-start(bf16[192,128,128]{2,1,0:T(8,128)(2,1)} %w_ref.1) | copy-start | bytes 18874372

commit v2 on v1

v2 whole, which is shorter than its diff:
```python
import functools

import jax
import jax.numpy as jnp
from jax import lax
from jax.experimental import pallas as pl
from jax.experimental.pallas import tpu as pltpu
from jax.sharding import PartitionSpec as P

MESH = pl.DeviceIdType.MESH
I32 = jnp.int32
F32 = jnp.float32
HALVES = 2
PARTS = 2
LEVELS = 32000.0
LOG2_E = 1.4426950408889634
EARLY = 8
PREP_ROWS = 8
ORDER = (0, 2, 6, 8, 1, 7, 3, 5)
SELF = 4


def steps(n):
    return n // 3 - 1, n % 3 - 1


def neighbour_keys(dev, tile, here_row, here_col, n_row, n_col, tiles):
    shift = n_col.bit_length() - 1
    rel_row = ((dev >> shift) - here_row) & (n_row - 1)
    rel_col = ((dev & (n_col - 1)) - here_col) & (n_col - 1)
    row_step = jnp.where(rel_row == n_row - 1, 0, jnp.where(rel_row == 0, 1, 2))
    col_step = jnp.where(rel_col == n_col - 1, 0, jnp.where(rel_col == 0, 1, 2))
    return (row_step * 3 + col_step) * tiles + tile


def sorted_order(key, src, tiles):
    count = key.shape[1]
    group = count // HALVES
    lane = lax.broadcasted_iota(I32, (1, count), 1)
    half = jnp.zeros_like(lane)
    for h in range(1, HALVES):
        half = half + (lane >= h * group).astype(I32)
    wide_key = half * 128 + key
    rank_row = wide_key * 256 + lane
    eye = lax.broadcasted_iota(I32, (count, count), 0) == lax.broadcasted_iota(
        I32, (count, count), 1
    )

    def column(row):
        return jnp.sum(jnp.where(eye, row, 0), axis=1, keepdims=True)

    rank_col = column(rank_row)
    src_col = column(src)
    place = jnp.sum((rank_row < rank_col).astype(I32), axis=1, keepdims=True)
    lanes = lax.broadcasted_iota(I32, (count, 256), 1)
    hit = place == lanes
    local = (rank_col & 255) - (rank_col >> 15) * group
    key_col = rank_col >> 8

    def arranged(col):
        return jnp.sum(jnp.where(hit, col, 0), axis=0, keepdims=True)

    rows = [arranged(local), arranged(src_col), arranged(key_col)]
    for h in range(HALVES):
        slot = lanes + h * 128
        inside = (key_col == slot) & (lanes < 128)
        upto = jnp.sum((key_col <= slot).astype(I32), axis=0, keepdims=True)
        some = jnp.sum(inside.astype(I32), axis=0, keepdims=True)
        rows.append(jnp.where(some > 0, upto - 1, -1))
    return rows


def pair_products(left, right):
    rows, cols = left[0].shape[0], right[0].shape[1]
    product = jnp.dot(
        jnp.concatenate(left, axis=0),
        jnp.concatenate(right, axis=1),
        preferred_element_type=F32,
    )
    return product[:rows, :cols], product[rows:, cols:]


def exchange(
    n_row,
    n_col,
    src_hbm,
    dev_hbm,
    tile_hbm,
    atm_hbm,
    w_hbm,
    state_hbm,
    mask_hbm,
    back_hbm,
    back_dev_hbm,
    back_tile_hbm,
    back_dst_hbm,
    import_ref,
    near_ref,
    back_ref,
    order_ref,
    src_ref,
    dev_ref,
    tile_ref,
    back_order,
    state_ref,
    mask_ref,
    small_sem,
    order_sem,
    back_sem,
    atm_v,
    *scratch,
):
    w_v = scratch[:HALVES]
    (
        sums,
        prep_v,
        prep_s,
        q_out,
            q_in,
        atm_sem,
        w_sem,
        prep_sem,
        send_sem,
        recv_sem,
        resp_send_sem,
        resp_recv_sem,
    ) = scratch[HALVES:]
    count = dev_ref.shape[1]
    group = count // HALVES
    tiles, fields, cells = state_ref.shape
    row = lax.axis_index("atm")
    col = lax.axis_index("ocn")

    def device(n):
        dr, dc = steps(n)
        return (lax.rem(row + dr + n_row, n_row), lax.rem(col + dc + n_col, n_col))

    def w_copy(h):
        return pltpu.make_async_copy(
            w_hbm.at[pl.ds(h * group, group)], w_v[h], w_sem.at[h]
        )

    w_copy(0).start()
    barrier = pltpu.get_barrier_semaphore()
    for n in ORDER:
        pl.semaphore_signal(barrier, inc=1, device_id=device(n), device_id_type=MESH)

    small_copies = [
        pltpu.make_async_copy(source, target, small_sem.at[i])
        for i, (source, target) in enumerate(
            (
                (src_hbm, src_ref),
                (dev_hbm, dev_ref),
                (tile_hbm, tile_ref),
                (state_hbm, state_ref),
                (mask_hbm, mask_ref),
                (back_dev_hbm, back_order.at[pl.ds(0, 1)]),
                (back_tile_hbm, back_order.at[pl.ds(1, 1)]),
                (back_dst_hbm, back_order.at[pl.ds(2, 1)]),
            )
        )
    ]
    for copy in small_copies[:3]:
        copy.start()
    atm_copy = pltpu.make_async_copy(atm_hbm, atm_v, atm_sem)
    atm_copy.start()
    for copy in small_copies[:3]:
        copy.wait()
    key = neighbour_keys(dev_ref[...], tile_ref[...], row, col, n_row, n_col, tiles)
    rows = sorted_order(key, src_ref[...], tiles)
    for i, values in enumerate(rows):
        prep_v[i : i + 1, :] = values
    prep_copy = pltpu.make_async_copy(prep_v, prep_s, prep_sem)
    prep_copy.start()
    for h in range(1, HALVES):
        w_copy(h).start()
    for copy in small_copies[3:]:
        copy.start()
    prep_copy.wait()
    atm_copy.wait()

    back_copy = pltpu.make_async_copy(back_hbm, back_ref, back_sem)
    for h in range(HALVES):
        w_copy(h).wait()

        def two(i, total, h=h):
            k = h * group + 2 * i
            products = pair_products(
                [atm_v[prep_s[1, k + side]] for side in range(2)],
                [w_v[h][prep_s[0, k + side]] for side in range(2)],
            )
            for side in range(2):
                before = prep_s[2, jnp.maximum(k + side - 1, 0)]
                same = (prep_s[2, k + side] == before) & (2 * i + side > 0)
                keep = jnp.where(same, 1.0, 0.0).astype(F32)
                total = total * keep + products[side]
                sums[k + side] = total
            return total

        lax.fori_loop(
            0, group // 2, two, jnp.zeros((fields, cells), F32), unroll=group // 2
        )

    def slot_sum(slot):
        total = None
        for h in range(HALVES):
            last = prep_s[3 + h, slot]
            part = sums[jnp.maximum(last, 0)] * jnp.where(last >= 0, 1.0, 0.0).astype(F32)
            total = part if total is None else total + part
        return total

    part = tiles // PARTS
    pair = part // 2
    values = pair * fields
    used = pl.ds(0, values + part)

    def encode(n, c):
        exponents = []
        levels = []
        for i in range(part):
            total = slot_sum(n * tiles + c * part + i)
            top = jnp.maximum(jnp.max(jnp.abs(total), axis=0, keepdims=True), 1e-30)
            exponent = jnp.ceil(jnp.log(top * (1.0 / LEVELS)) * LOG2_E)
            levels.append(jnp.round(total * jnp.exp2(-exponent)).astype(I32))
            exponents.append(exponent.astype(I32))
        for i in range(pair):
            packed = (levels[i] << 16) | (levels[i + pair] & 0xFFFF)
            q_out[c, n, i * fields : (i + 1) * fields] = packed
        for i in range(part):
            q_out[c, n, values + i : values + i + 1] = exponents[i]

    arriving = []

    def send(n, c):
        copy = pltpu.make_async_remote_copy(
            src_ref=q_out.at[c, n, used],
            dst_ref=q_in.at[c, 8 - n, used],
            send_sem=send_sem.at[c, n],
            recv_sem=recv_sem.at[c, 8 - n],
            device_id=device(n),
            device_id_type=MESH,
        )
        copy.start()
        arriving[c].append(copy)

    for n in ORDER[:EARLY]:
        encode(n, 0)
    pl.semaphore_wait(barrier, 8)
    for c in range(PARTS):
        arriving.append([])
        for i, n in enumerate(ORDER):
            if c > 0 or i >= EARLY:
                encode(n, c)
            send(n, c)
    back_copy.start()
    for t in range(tiles):
        import_ref[t] = slot_sum(SELF * tiles + t)
    for copy in small_copies[3:]:
        copy.wait()
    back_order[0:1] = neighbour_keys(
        back_order[0:1], back_order[1:2], row, col, n_row, n_col, tiles
    )
    order_copy = pltpu.make_async_copy(back_order, order_ref, order_sem)
    order_copy.start()

    answers = []
    for c in range(PARTS):
        span = pl.ds(c * part, part)
        for copy in arriving[c]:
            copy.wait_recv()
        for i in range(part):
            t = c * part + i
            total = import_ref[t]
            for n in ORDER:
                packed = q_in[c, n, (i % pair) * fields : (i % pair + 1) * fields]
                level = packed >> 16 if i < pair else (packed << 16) >> 16
                exponent = q_in[c, n, values + i : values + i + 1].astype(F32)
                total = total + level.astype(F32) * jnp.exp2(exponent)
            import_ref[t] = total
            wet = mask_ref[t : t + 1].astype(F32)
            near_ref[SELF, t] = (wet * jnp.tanh(state_ref[t] + total)).astype(jnp.bfloat16)
        for n in ORDER:
            copy = pltpu.make_async_remote_copy(
                src_ref=near_ref.at[SELF, span],
                dst_ref=near_ref.at[8 - n, span],
                send_sem=resp_send_sem.at[c, n],
                recv_sem=resp_recv_sem.at[c, 8 - n],
                device_id=device(n),
                device_id_type=MESH,
            )
            copy.start()
            answers.append(copy)
    back_copy.wait()
    order_copy.wait()
    for copies in arriving:
        for copy in copies:
            copy.wait_send()
    for copy in answers:
        copy.wait()


def backward(order_ref, near_ref, import_ref, w_ref, imported_ref, out_ref):
    count = order_ref.shape[1]
    atmos, fields, cells = out_ref.shape
    imported_ref[...] = import_ref[...]

    def clear(t, _):
        out_ref[t] = jnp.zeros((fields, cells), F32)
        return 0

    lax.fori_loop(0, atmos, clear, 0, unroll=atmos)

    def two(i, _):
        b = 2 * i
        products = pair_products(
            [near_ref[order_ref[0, b + side]] for side in range(2)],
            [w_ref[b + side] for side in range(2)],
        )
        for side in range(2):
            dst = order_ref[2, b + side]
            out_ref[dst] = out_ref[dst] + products[side]
        return 0

    lax.fori_loop(0, count // 2, two, 0, unroll=count // 2)


def shards(
    atm_fields,
    fwd_blocks,
    fwd_src_tile,
    fwd_dst_dev,
    fwd_dst_tile,
    ocean_state,
    wet_mask,
    back_blocks,
    back_src_dev,
    back_src_tile,
    back_dst_tile,
):
    n_row = lax.axis_size("atm")
    n_col = lax.axis_size("ocn")
    blocks, cells, _ = fwd_blocks.shape
    group = blocks // HALVES
    atmos, fields, _ = atm_fields.shape
    tiles = ocean_state.shape[0]
    rows = tiles // PARTS // 2 * fields + 8
    vmem = pl.BlockSpec(memory_space=pltpu.VMEM)
    smem = pl.BlockSpec(memory_space=pltpu.SMEM)
    hbm = pl.BlockSpec(memory_space=pltpu.HBM)
    ocean_import, near, back_near, order = pl.pallas_call(
        functools.partial(exchange, n_row, n_col),
        out_shape=(
            jax.ShapeDtypeStruct((tiles, fields, cells), F32),
            jax.ShapeDtypeStruct((9, tiles, fields, cells), jnp.bfloat16),
            jax.ShapeDtypeStruct((blocks, cells, cells), jnp.bfloat16),
            pltpu.SMEM((3, blocks), I32),
        ),
        in_specs=[hbm] * 11,
        out_specs=(vmem, vmem, vmem, smem),
        scratch_shapes=[
            pltpu.VMEM((1, blocks), I32),
            pltpu.VMEM((1, blocks), I32),
            pltpu.VMEM((1, blocks), I32),
            pltpu.VMEM((3, blocks), I32),
            pltpu.VMEM((tiles, fields, cells), F32),
            pltpu.VMEM((tiles, cells), I32),
            pltpu.SemaphoreType.DMA((8,)),
            pltpu.SemaphoreType.DMA,
            pltpu.SemaphoreType.DMA,
            pltpu.VMEM((atmos, fields, cells), jnp.bfloat16),
            *[pltpu.VMEM((group, cells, cells), jnp.bfloat16)] * HALVES,
            pltpu.VMEM((blocks, fields, cells), F32),
            pltpu.VMEM((PREP_ROWS, 256), I32),
            pltpu.SMEM((PREP_ROWS, 256), I32),
            pltpu.VMEM((PARTS, 9, rows, cells), I32),
            pltpu.VMEM((PARTS, 9, rows, cells), I32),
            pltpu.SemaphoreType.DMA,
            pltpu.SemaphoreType.DMA((HALVES,)),
            pltpu.SemaphoreType.DMA,
            *[pltpu.SemaphoreType.DMA((PARTS, 9))] * 4,
        ],
        compiler_params=pltpu.CompilerParams(
            collective_id=0, has_side_effects=True, vmem_limit_bytes=28 * 2**20
        ),
        name="exchange",
    )(
        *[
            pltpu.with_memory_space_constraint(operand, pltpu.HBM)
            for operand in (
                fwd_src_tile.reshape(1, blocks),
                fwd_dst_dev.reshape(1, blocks),
                fwd_dst_tile.reshape(1, blocks),
                atm_fields,
                fwd_blocks,
                ocean_state,
                wet_mask,
                back_blocks,
                back_src_dev.reshape(1, blocks),
                back_src_tile.reshape(1, blocks),
                back_dst_tile.reshape(1, blocks),
            )
        ]
    )
    return pl.pallas_call(
        backward,
        out_shape=(
            jax.ShapeDtypeStruct((tiles, fields, cells), F32),
            jax.ShapeDtypeStruct((atmos, fields, cells), F32),
        ),
        in_specs=[smem, vmem, vmem, vmem],
        out_specs=(vmem, vmem),
        compiler_params=pltpu.CompilerParams(vmem_limit_bytes=28 * 2**20),
        name="backward",
    )(
        pltpu.with_memory_space_constraint(order, pltpu.SMEM),
        near.reshape(9 * tiles, fields, cells),
        ocean_import,
        back_near,
    )


def solution(mesh):
    both = ("atm", "ocn")
    in_specs = (
        P(both, None, None),
        P(both, None, None),
        P(both),
        P(both, None),
        P(both),
        P(both, None, None),
        P(both, None),
        P(both, None, None),
        P(both, None),
        P(both),
        P(both),
    )
    out_specs = (P(both, None, None), P(both, None, None))
    return jax.shard_map(shards, mesh=mesh, in_specs=in_specs, out_specs=out_specs, check_vma=False)
```

time: 31.1 us -> 25 us (0.80)
  Pallas kernels: 30.3 us -> 24.2 us
    pallas_call x1, Pallas kernels: 6.36 us -> 2.46 us  [shards(): pl.pallas_call(backward, out_shape=(jax.ShapeDtypeStruct((tiles, fields,...]
    pallas_call x1, Pallas kernels: 24 us -> 21.8 us  [shards(): pl.pallas_call(functools.partial(exchange, n_row, n_col), out_shape=(jax....]
where the time goes in v2:
time: 25 us; the launch traced here: 24.9 us
  Pallas kernels  24.2 us (97%)
  between operations  0.64 us (3%)
    pallas_call x1, Pallas kernels, shards(): pl.pallas_call(functools.partial(exchange, n_row, n_col), out_shape=(jax....  21.8 us
    pallas_call x1, Pallas kernels, shards(): pl.pallas_call(backward, out_shape=(jax.ShapeDtypeStruct((tiles, fields,...  2.46 us

profile of v2, /device:TPU:1, one launch (start us, length us, event | category | flops | bytes accessed | tf_op | source)
XLA Modules:
  0.0 24.9 jit_solution(9914641969828125670)
XLA Ops:
  0.6 21.8 %exchange.1 = (f32[8,24,128]{2,1,0:T(8,128)S(1)}, bf16[9,8,24,128]{3,2,1,0:T(8,128)(2,1)S(1)}, bf16[192,128,128]{2,1,0:T(8,128)(2,1)S(1)}, s32[3,192]{1,0:T(4,128)S(4)}) custom-call(s32[1,192]{1,0:T(1,128)} %bitcast.8, s32[1,192]{1,0:T(1,128)} %bitcast.9, s32[1,192]{1,0:T(1,128)} %bitcast.10, bf16[128,24,128]{2,1,0:T(8,128)(2,1)} %atm_hbm.1, ...), custom_call_target="tpu_custom_call" | custom-call | tf_op jit(solution)/shard_map/exchange/pallas_call | solution.py:350
  22.4 2.5 %backward.1 = (f32[8,24,128]{2,1,0:T(8,128)}, f32[128,24,128]{2,1,0:T(8,128)}) custom-call(s32[3,192]{1,0:T(4,128)S(4)} %get-tuple-element.6.order_ref, bf16[72,24,128]{2,1,0:T(8,128)(2,1)S(1)} %bitcast.7, f32[8,24,128]{2,1,0:T(8,128)S(1)} %get-tuple-element.8.import_ref, bf16[192,128,128]{2,1,0:T(8,128)(2,1)S(1)} %get-tuple-element.9.w_ref), custom_call_target="tpu_custom_call" | custom-call | tf_op jit(solution)/shard_map/backward/pallas_call | solution.py:404

commit v3 on v2

--- a/solution.py
+++ b/solution.py
@@ -14,7 +14,6 @@
 PARTS = 2
 LEVELS = 32000.0
 LOG2_E = 1.4426950408889634
-EARLY = 8
 PREP_ROWS = 8
 ORDER = (0, 2, 6, 8, 1, 7, 3, 5)
 SELF = 4
@@ -140,11 +139,11 @@
             w_hbm.at[pl.ds(h * group, group)], w_v[h], w_sem.at[h]
         )
 
-    w_copy(0).start()
     barrier = pltpu.get_barrier_semaphore()
     for n in ORDER:
         pl.semaphore_signal(barrier, inc=1, device_id=device(n), device_id_type=MESH)
 
+    w_copy(0).start()
     small_copies = [
         pltpu.make_async_copy(source, target, small_sem.at[i])
         for i, (source, target) in enumerate(
@@ -243,14 +242,13 @@
         copy.start()
         arriving[c].append(copy)
 
-    for n in ORDER[:EARLY]:
-        encode(n, 0)
+    for c in range(PARTS):
+        for n in ORDER:
+            encode(n, c)
     pl.semaphore_wait(barrier, 8)
     for c in range(PARTS):
         arriving.append([])
-        for i, n in enumerate(ORDER):
-            if c > 0 or i >= EARLY:
-                encode(n, c)
+        for n in ORDER:
             send(n, c)
     back_copy.start()
     for t in range(tiles):
@@ -266,19 +264,17 @@
     answers = []
     for c in range(PARTS):
         span = pl.ds(c * part, part)
-        for copy in arriving[c]:
+        for n, copy in zip(ORDER[::-1], arriving[c][::-1]):
             copy.wait_recv()
+            for i in range(part):
+                packed = q_in[c, 8 - n, (i % pair) * fields : (i % pair + 1) * fields]
+                level = packed >> 16 if i < pair else (packed << 16) >> 16
+                exponent = q_in[c, 8 - n, values + i : values + i + 1].astype(F32)
+                import_ref[c * part + i] = import_ref[c * part + i] + level.astype(F32) * jnp.exp2(exponent)
         for i in range(part):
             t = c * part + i
-            total = import_ref[t]
-            for n in ORDER:
-                packed = q_in[c, n, (i % pair) * fields : (i % pair + 1) * fields]
-                level = packed >> 16 if i < pair else (packed << 16) >> 16
-                exponent = q_in[c, n, values + i : values + i + 1].astype(F32)
-                total = total + level.astype(F32) * jnp.exp2(exponent)
-            import_ref[t] = total
             wet = mask_ref[t : t + 1].astype(F32)
-            near_ref[SELF, t] = (wet * jnp.tanh(state_ref[t] + total)).astype(jnp.bfloat16)
+            near_ref[SELF, t] = (wet * jnp.tanh(state_ref[t] + import_ref[t])).astype(jnp.bfloat16)
         for n in ORDER:
             copy = pltpu.make_async_remote_copy(
                 src_ref=near_ref.at[SELF, span],

time: 25 us -> 24.9 us (level)
  no operation moved by 1% of the time
where the time goes in v3:
time: 24.9 us; the launch traced here: 24.8 us
  Pallas kernels  24.1 us (97%)
  between operations  0.64 us (3%)
    pallas_call x1, Pallas kernels, shards(): pl.pallas_call(functools.partial(exchange, n_row, n_col), out_shape=(jax....  21.7 us
    pallas_call x1, Pallas kernels, shards(): pl.pallas_call(backward, out_shape=(jax.ShapeDtypeStruct((tiles, fields,...  2.47 us

profile of v3, /device:TPU:1, one launch (start us, length us, event | category | flops | bytes accessed | tf_op | source)
XLA Modules:
  0.0 24.8 jit_solution(15674275520753217361)
XLA Ops:
  0.6 21.7 %exchange.1 = (f32[8,24,128]{2,1,0:T(8,128)S(1)}, bf16[9,8,24,128]{3,2,1,0:T(8,128)(2,1)S(1)}, bf16[192,128,128]{2,1,0:T(8,128)(2,1)S(1)}, s32[3,192]{1,0:T(4,128)S(4)}) custom-call(s32[1,192]{1,0:T(1,128)} %bitcast.8, s32[1,192]{1,0:T(1,128)} %bitcast.9, s32[1,192]{1,0:T(1,128)} %bitcast.10, bf16[128,24,128]{2,1,0:T(8,128)(2,1)} %atm_hbm.1, ...), custom_call_target="tpu_custom_call" | custom-call | tf_op jit(solution)/shard_map/exchange/pallas_call | solution.py:346
  22.3 2.5 %backward.1 = (f32[8,24,128]{2,1,0:T(8,128)}, f32[128,24,128]{2,1,0:T(8,128)}) custom-call(s32[3,192]{1,0:T(4,128)S(4)} %get-tuple-element.6.order_ref, bf16[72,24,128]{2,1,0:T(8,128)(2,1)S(1)} %bitcast.7, f32[8,24,128]{2,1,0:T(8,128)S(1)} %get-tuple-element.8.import_ref, bf16[192,128,128]{2,1,0:T(8,128)(2,1)S(1)} %get-tuple-element.9.w_ref), custom_call_target="tpu_custom_call" | custom-call | tf_op jit(solution)/shard_map/backward/pallas_call | solution.py:400

commit v4 on v3

--- a/solution.py
+++ b/solution.py
@@ -77,6 +77,25 @@
         preferred_element_type=F32,
     )
     return product[:rows, :cols], product[rows:, cols:]
+
+
+def by_destination(slot, dst):
+    count = dst.shape[1]
+    square = (count, count)
+    lane = lax.broadcasted_iota(I32, square, 1)
+    eye = lax.broadcasted_iota(I32, square, 0) == lane
+    rank_row = dst * 256 + lane[:1]
+
+    def column(row):
+        return jnp.sum(jnp.where(eye, row, 0), axis=1, keepdims=True)
+
+    rank_col = column(rank_row)
+    place = jnp.sum((rank_row < rank_col).astype(I32), axis=1, keepdims=True)
+    hit = place == lane
+    return [
+        jnp.sum(jnp.where(hit, col, 0), axis=0, keepdims=True)
+        for col in (column(slot), rank_col & 255, rank_col >> 8)
+    ]
 
 
 def exchange(
@@ -255,9 +274,11 @@
         import_ref[t] = slot_sum(SELF * tiles + t)
     for copy in small_copies[3:]:
         copy.wait()
-    back_order[0:1] = neighbour_keys(
+    slots = neighbour_keys(
         back_order[0:1], back_order[1:2], row, col, n_row, n_col, tiles
     )
+    for i, values_row in enumerate(by_destination(slots, back_order[2:3])):
+        back_order[i : i + 1] = values_row
     order_copy = pltpu.make_async_copy(back_order, order_ref, order_sem)
     order_copy.start()
 
@@ -295,10 +316,11 @@
         copy.wait()
 
 
-def backward(order_ref, near_ref, import_ref, w_ref, imported_ref, out_ref):
+def backward(order_ref, near_ref, import_ref, w_ref, imported_hbm, out_hbm, out_ref, sem):
     count = order_ref.shape[1]
     atmos, fields, cells = out_ref.shape
-    imported_ref[...] = import_ref[...]
+    import_copy = pltpu.make_async_copy(import_ref, imported_hbm, sem.at[0])
+    import_copy.start()
 
     def clear(t, _):
         out_ref[t] = jnp.zeros((fields, cells), F32)
@@ -310,14 +332,32 @@
         b = 2 * i
         products = pair_products(
             [near_ref[order_ref[0, b + side]] for side in range(2)],
-            [w_ref[b + side] for side in range(2)],
+            [w_ref[order_ref[1, b + side]] for side in range(2)],
         )
         for side in range(2):
             dst = order_ref[2, b + side]
             out_ref[dst] = out_ref[dst] + products[side]
         return 0
 
-    lax.fori_loop(0, count // 2, two, 0, unroll=count // 2)
+    quarter = atmos // 4
+    out_copies = [
+        pltpu.make_async_copy(
+            out_ref.at[pl.ds(q * quarter, quarter)],
+            out_hbm.at[pl.ds(q * quarter, quarter)],
+            sem.at[1 + q],
+        )
+        for q in range(4)
+    ]
+    first = count // 3
+    lax.fori_loop(0, first, two, 0, unroll=first)
+    ready = order_ref[2, 2 * first]
+    for q, copy in enumerate(out_copies):
+        pl.when(ready >= (q + 1) * quarter)(copy.start)
+    lax.fori_loop(first, count // 2, two, 0, unroll=count // 2 - first)
+    for q, copy in enumerate(out_copies):
+        pl.when(ready < (q + 1) * quarter)(copy.start)
+    for copy in [import_copy, *out_copies]:
+        copy.wait()
 
 
 def shards(
@@ -404,7 +444,11 @@
             jax.ShapeDtypeStruct((atmos, fields, cells), F32),
         ),
         in_specs=[smem, vmem, vmem, vmem],
-        out_specs=(vmem, vmem),
+        out_specs=(hbm, hbm),
+        scratch_shapes=[
+            pltpu.VMEM((atmos, fields, cells), F32),
+            pltpu.SemaphoreType.DMA((5,)),
+        ],
         compiler_params=pltpu.CompilerParams(vmem_limit_bytes=28 * 2**20),
         name="backward",
     )(

time: 24.9 us -> 24.8 us (level)
  no operation moved by 1% of the time
where the time goes in v4:
time: 24.8 us; the launch traced here: 24.7 us
  Pallas kernels  24 us (97%)
  between operations  0.64 us (3%)
    pallas_call x1, Pallas kernels, shards(): pl.pallas_call(functools.partial(exchange, n_row, n_col), out_shape=(jax....  21.7 us
    pallas_call x1, Pallas kernels, shards(): pl.pallas_call(backward, out_shape=(jax.ShapeDtypeStruct((tiles, fields,...  2.38 us

profile of v4, /device:TPU:1, one launch (start us, length us, event | category | flops | bytes accessed | tf_op | source)
XLA Modules:
  0.0 24.7 jit_solution(10946720594948900204)
XLA Ops:
  0.6 21.7 %exchange.1 = (f32[8,24,128]{2,1,0:T(8,128)S(1)}, bf16[9,8,24,128]{3,2,1,0:T(8,128)(2,1)S(1)}, bf16[192,128,128]{2,1,0:T(8,128)(2,1)S(1)}, s32[3,192]{1,0:T(4,128)S(4)}) custom-call(s32[1,192]{1,0:T(1,128)} %bitcast.8, s32[1,192]{1,0:T(1,128)} %bitcast.9, s32[1,192]{1,0:T(1,128)} %bitcast.10, bf16[128,24,128]{2,1,0:T(8,128)(2,1)} %atm_hbm.1, ...), custom_call_target="tpu_custom_call" | custom-call | tf_op jit(solution)/shard_map/exchange/pallas_call | solution.py:386
  22.3 2.4 %backward.1 = (f32[8,24,128]{2,1,0:T(8,128)}, f32[128,24,128]{2,1,0:T(8,128)}) custom-call(s32[3,192]{1,0:T(4,128)S(4)} %get-tuple-element.6.order_ref, bf16[72,24,128]{2,1,0:T(8,128)(2,1)S(1)} %bitcast.7, f32[8,24,128]{2,1,0:T(8,128)S(1)} %get-tuple-element.8.import_ref, bf16[192,128,128]{2,1,0:T(8,128)(2,1)S(1)} %get-tuple-element.9.w_ref), custom_call_target="tpu_custom_call" | custom-call | tf_op jit(solution)/shard_map/backward/pallas_call | solution.py:440

commit v5 on v4

--- a/solution.py
+++ b/solution.py
@@ -17,6 +17,7 @@
 PREP_ROWS = 8
 ORDER = (0, 2, 6, 8, 1, 7, 3, 5)
 SELF = 4
+SHARES = 8
 
 
 def steps(n):
@@ -339,23 +340,23 @@
             out_ref[dst] = out_ref[dst] + products[side]
         return 0
 
-    quarter = atmos // 4
+    share = atmos // SHARES
     out_copies = [
         pltpu.make_async_copy(
-            out_ref.at[pl.ds(q * quarter, quarter)],
-            out_hbm.at[pl.ds(q * quarter, quarter)],
+            out_ref.at[pl.ds(q * share, share)],
+            out_hbm.at[pl.ds(q * share, share)],
             sem.at[1 + q],
         )
-        for q in range(4)
+        for q in range(SHARES)
     ]
-    first = count // 3
+    first = count * 3 // 8
     lax.fori_loop(0, first, two, 0, unroll=first)
     ready = order_ref[2, 2 * first]
     for q, copy in enumerate(out_copies):
-        pl.when(ready >= (q + 1) * quarter)(copy.start)
+        pl.when(ready >= (q + 1) * share)(copy.start)
     lax.fori_loop(first, count // 2, two, 0, unroll=count // 2 - first)
     for q, copy in enumerate(out_copies):
-        pl.when(ready < (q + 1) * quarter)(copy.start)
+        pl.when(ready < (q + 1) * share)(copy.start)
     for copy in [import_copy, *out_copies]:
         copy.wait()
 
@@ -447,7 +448,7 @@
         out_specs=(hbm, hbm),
         scratch_shapes=[
             pltpu.VMEM((atmos, fields, cells), F32),
-            pltpu.SemaphoreType.DMA((5,)),
+            pltpu.SemaphoreType.DMA((1 + SHARES,)),
         ],
         compiler_params=pltpu.CompilerParams(vmem_limit_bytes=28 * 2**20),
         name="backward",

time: 24.8 us -> 24.8 us (level)
  no operation moved by 1% of the time
where the time goes in v5:
time: 24.8 us; the launch traced here: 24.7 us
  Pallas kernels  24 us (97%)
  between operations  0.64 us (3%)
    pallas_call x1, Pallas kernels, shards(): pl.pallas_call(functools.partial(exchange, n_row, n_col), out_shape=(jax....  21.7 us
    pallas_call x1, Pallas kernels, shards(): pl.pallas_call(backward, out_shape=(jax.ShapeDtypeStruct((tiles, fields,...  2.38 us

profile of v5, /device:TPU:1, one launch (start us, length us, event | category | flops | bytes accessed | tf_op | source)
XLA Modules:
  0.0 24.7 jit_solution(16179491753833151250)
XLA Ops:
  0.6 21.7 %exchange.1 = (f32[8,24,128]{2,1,0:T(8,128)S(1)}, bf16[9,8,24,128]{3,2,1,0:T(8,128)(2,1)S(1)}, bf16[192,128,128]{2,1,0:T(8,128)(2,1)S(1)}, s32[3,192]{1,0:T(4,128)S(4)}) custom-call(s32[1,192]{1,0:T(1,128)} %bitcast.8, s32[1,192]{1,0:T(1,128)} %bitcast.9, s32[1,192]{1,0:T(1,128)} %bitcast.10, bf16[128,24,128]{2,1,0:T(8,128)(2,1)} %atm_hbm.1, ...), custom_call_target="tpu_custom_call" | custom-call | tf_op jit(solution)/shard_map/exchange/pallas_call | solution.py:387
  22.3 2.4 %backward.1 = (f32[8,24,128]{2,1,0:T(8,128)}, f32[128,24,128]{2,1,0:T(8,128)}) custom-call(s32[3,192]{1,0:T(4,128)S(4)} %get-tuple-element.6.order_ref, bf16[72,24,128]{2,1,0:T(8,128)(2,1)S(1)} %bitcast.7, f32[8,24,128]{2,1,0:T(8,128)S(1)} %get-tuple-element.8.import_ref, bf16[192,128,128]{2,1,0:T(8,128)(2,1)S(1)} %get-tuple-element.9.w_ref), custom_call_target="tpu_custom_call" | custom-call | tf_op jit(solution)/shard_map/backward/pallas_call | solution.py:441
